TPU v7x, 256 devices: a whole 4x4x8 slice. The times are simulated.
256 devices in a mesh: dp: 32 (over z, x), tensor: 8 (over y, core).
Axes of the slice: x: 4, y: 4, z: 8, core: 2. Of those that a mesh axis runs over, the one named last changes fastest.
Arguments:
- queries: bfloat16 [512, 128, 4096], P(('dp', 'tensor')), may hold values from -5 to 5, as said below
- keys: bfloat16 [512, 128, 1024], P(('dp', 'tensor')), may hold values from -5 to 5, as said below
- values: bfloat16 [512, 128, 1024], P(('dp', 'tensor')), may hold values from -6 to 6
- out_grad: bfloat16 [512, 128, 4096], P(('dp', 'tensor')), may hold values from -24 to 24
- out_weight: bfloat16 [4096, 4096], P('tensor'), may hold values from -0.09375 to 0.09375
- lengths: int32 [512], P(('dp', 'tensor')), may hold values from 4 to 124, as said below
- dest_group: int32 [512], P(('dp', 'tensor')), may hold values from 0 to 31, as said below
- dest_offset: int32 [512], P(('dp', 'tensor')), may hold values from 0 to 124, as said below
Outputs:
- query_grad: bfloat16 [32768, 4096], P(('dp', 'tensor'))
- key_grad: bfloat16 [32768, 1024], P(('dp', 'tensor'))
- value_grad: bfloat16 [32768, 1024], P(('dp', 'tensor'))
- weight_grad: float32 [4096, 4096], P('tensor', 'dp')
Inputs may be any that keep to these rules, and one draw needn't show every extreme that they name: queries of order one. keys of order one. Slot r holds a rollout row of lengths[r] tokens at its start; the rest of the slot is padding. `dest_group`: a row's destination group is its own index along dp or the one 32 // 2 away; it keeps its index along tensor. Every device receives exactly 2 rows, whose lengths sum to 128. `dest_offset`: the rows packed into one device don't intersect and fill its 128 positions.
All inputs are finite; a program needn't handle non-finite values.
Results may differ from a plain program's by a relative error of at most 0.027.
Values may be sent and summed in bfloat16 or wider, within the bound.
A program may use at most 128 MiB of HBM per device.

v0:
```python
import jax
import jax.numpy as jnp
from jax import lax
from jax.sharding import PartitionSpec as P

HEAD_DIM = 128


def passed_along(array, axis, by):
    devices = lax.axis_size(axis)
    return lax.ppermute(array, axis, [(i, (i + by) % devices) for i in range(devices)])


def place_rows(block, offset):
    span = block.shape[0]
    padded = jnp.concatenate([jnp.zeros_like(block), block], axis=0)
    return lax.dynamic_slice_in_dim(padded, (span - offset).astype(jnp.int32), span, 0)


def pack_rows(fields, mask, tag_base, offsets):
    members = mask.shape[0]
    span = mask.shape[1]
    posit = jnp.arange(span, dtype=jnp.int32)
    placed = []
    for field in fields:
        total = jnp.zeros_like(field[0])
        for member in range(members):
            kept = jnp.where(mask[member][:, None], field[member], jnp.zeros_like(field[member]))
            total = total + place_rows(kept, offsets[member])
        placed.append(total)
    labels = jnp.zeros((span,), jnp.int32)
    positions = jnp.zeros((span,), jnp.int32)
    for member in range(members):
        tag = jnp.where(mask[member], member + tag_base, 0).astype(jnp.int32)
        labels = labels + place_rows(tag, offsets[member])
        positions = positions + place_rows(jnp.where(mask[member], posit, 0), offsets[member])
    return (tuple(placed), labels, positions)


def group_probs(query_grp, key_grp, labels, positions, scale):
    scores = (
        jnp.einsum("gickd,gjcd->gckij", query_grp, key_grp, preferred_element_type=jnp.float32)
        * scale
    )
    allowed = (labels[:, :, None] == labels[:, None, :]) & (
        positions[:, None, :] <= positions[:, :, None]
    )
    allowed = allowed[:, None, None]
    top = jnp.max(jnp.where(allowed, scores, -1e30), axis=-1, keepdims=True)
    expo = jnp.where(allowed, jnp.exp(scores - top), 0.0)
    return expo / jnp.sum(expo, axis=-1, keepdims=True)


def local(queries, keys, values, out_grad, out_weight, lengths, dest_group, dest_offset):
    span = queries.shape[1]
    n_tensor = lax.axis_size("tensor")
    n_data = lax.axis_size("dp")
    half = n_data // 2
    own_group = lax.axis_index("dp")
    posit = jnp.arange(span, dtype=jnp.int32)
    valid = posit[None, :] < lengths[:, None]
    moving = dest_group != own_group
    keep_mask = valid & jnp.logical_not(moving)[:, None]
    move_mask = valid & moving[:, None]
    fields = (queries, keys, values, out_grad)
    own_fields, own_labels, own_positions = pack_rows(fields, keep_mask, 1, dest_offset)
    moved = tuple(
        (jnp.where(move_mask[:, :, None], field, jnp.zeros_like(field)) for field in fields)
    )
    moved_lengths = jnp.where(moving, lengths, 0)
    arrived = passed_along(
        (moved[0], moved[1], moved[2], moved[3], moved_lengths, dest_offset), "dp", half
    )
    arrive_mask = posit[None, :] < arrived[4][:, None]
    got_fields, got_labels, got_positions = pack_rows(arrived[0:4], arrive_mask, 3, arrived[5])
    dest_fields = tuple((own_fields[index_f] + got_fields[index_f] for index_f in range(4)))
    labels = own_labels + got_labels
    positions = own_positions + got_positions
    label_wide = jnp.broadcast_to(labels[:, None], (span, n_tensor))
    position_wide = jnp.broadcast_to(positions[:, None], (span, n_tensor))
    head_query, head_key, head_value, head_label, head_position = (
        lax.all_to_all(dest_fields[0], "tensor", split_axis=1, concat_axis=0, tiled=True),
        lax.all_to_all(dest_fields[1], "tensor", split_axis=1, concat_axis=0, tiled=True),
        lax.all_to_all(dest_fields[2], "tensor", split_axis=1, concat_axis=0, tiled=True),
        lax.all_to_all(label_wide, "tensor", split_axis=1, concat_axis=0, tiled=True),
        lax.all_to_all(position_wide, "tensor", split_axis=1, concat_axis=0, tiled=True),
    )
    rows_all = n_tensor * span
    group_label = head_label[:, 0].reshape(n_tensor, span)
    group_position = head_position[:, 0].reshape(n_tensor, span)
    scale = float(HEAD_DIM) ** (-0.5)
    local_heads = head_query.shape[1] // HEAD_DIM
    local_kv = head_key.shape[1] // HEAD_DIM
    group_size = local_heads // local_kv
    query_grp = head_query.reshape(n_tensor, span, local_kv, group_size, HEAD_DIM)
    key_grp = head_key.reshape(n_tensor, span, local_kv, HEAD_DIM)
    value_grp = head_value.reshape(n_tensor, span, local_kv, HEAD_DIM)
    probs = group_probs(query_grp, key_grp, group_label, group_position, scale)
    probs_b = probs.astype(jnp.bfloat16)
    attended_grp = jnp.einsum(
        "gckij,gjcd->gickd", probs_b, value_grp, preferred_element_type=jnp.float32
    )
    attended_all = attended_grp.astype(jnp.bfloat16).reshape(rows_all, local_heads * HEAD_DIM)
    piece = lax.all_gather(dest_fields[3], "tensor", axis=0, tiled=True)
    part_grad = lax.dot_general(
        piece, out_weight, (((1,), (1,)), ((), ())), preferred_element_type=jnp.float32
    )
    weight_term = lax.dot_general(
        attended_all, piece, (((0,), (0,)), ((), ())), preferred_element_type=jnp.float32
    )
    att_grad_f, weight_term = (part_grad, weight_term)
    att_grad = att_grad_f.astype(jnp.bfloat16)
    grad_grp = att_grad.reshape(n_tensor, span, local_kv, group_size, HEAD_DIM)
    att_grp = attended_all.reshape(n_tensor, span, local_kv, group_size, HEAD_DIM)
    delta = jnp.sum(grad_grp.astype(jnp.float32) * att_grp.astype(jnp.float32), axis=-1).transpose(
        0, 2, 3, 1
    )
    prob_grad = jnp.einsum(
        "gickd,gjcd->gckij", grad_grp, value_grp, preferred_element_type=jnp.float32
    )
    score_b = (probs * (prob_grad - delta[..., None])).astype(jnp.bfloat16)
    query_g = (
        jnp.einsum("gckij,gjcd->gickd", score_b, key_grp, preferred_element_type=jnp.float32)
        * scale
    )
    key_g = (
        jnp.einsum("gckij,gickd->gjcd", score_b, query_grp, preferred_element_type=jnp.float32)
        * scale
    )
    value_g = jnp.einsum("gckij,gickd->gjcd", probs_b, grad_grp, preferred_element_type=jnp.float32)
    query_heads = query_g.astype(jnp.bfloat16).reshape(rows_all, local_heads * HEAD_DIM)
    key_heads = key_g.astype(jnp.bfloat16).reshape(rows_all, local_kv * HEAD_DIM)
    value_heads = value_g.astype(jnp.bfloat16).reshape(rows_all, local_kv * HEAD_DIM)
    query_grad, key_grad, value_grad = (
        lax.all_to_all(query_heads, "tensor", split_axis=0, concat_axis=1, tiled=True),
        lax.all_to_all(key_heads, "tensor", split_axis=0, concat_axis=1, tiled=True),
        lax.all_to_all(value_heads, "tensor", split_axis=0, concat_axis=1, tiled=True),
    )
    weight_grad = lax.psum_scatter(
        weight_term.astype(jnp.bfloat16), "dp", scatter_dimension=1, tiled=True
    ).astype(jnp.float32)
    return (query_grad, key_grad, value_grad, weight_grad)


def solution(mesh):
    in_specs = (
        P(("dp", "tensor"), None, None),
        P(("dp", "tensor"), None, None),
        P(("dp", "tensor"), None, None),
        P(("dp", "tensor"), None, None),
        P("tensor", None),
        P(("dp", "tensor")),
        P(("dp", "tensor")),
        P(("dp", "tensor")),
    )
    out_specs = (
        P(("dp", "tensor"), None),
        P(("dp", "tensor"), None),
        P(("dp", "tensor"), None),
        P("tensor", "dp"),
    )
    return jax.shard_map(local, mesh=mesh, in_specs=in_specs, out_specs=out_specs, check_vma=False)
```

profile of v0, /device:TPU:1, one launch (start us, length us, event | category | flops | bytes accessed | tf_op | source)
XLA Modules:
  0.0 577.7 jit_solution(14396715286069953013)
XLA Ops:
  8.6 4.8 broadcast_select_fusion.1
  13.4 7.7 %collective-permute-start.3 = (bf16[2,128,4096]{2,1,0:T(8,128)(2,1)}, bf16[2,128,4096]{2,1,0:T(8,128)(2,1)}, u32[]{:S(2)}, u32[]{:S(2)}) collective-permute-start(bf16[2,128,4096]{2,1,0:T(8,128)(2,1)} %get-tuple-element.52), channel_id=1, source_target_pairs={{0,128},{8,136},{16,144},{24,152},{32,160},{40,168},{48,176},{56,1... | collective-permute-start | bytes 6291464 | tf_op jit(solution)/shard_map/ppermute | solution.py:11
  21.2 5.3 collective-permute-start
  29.8 3.4 bitcast_select_fusion.1
  33.1 141.2 %collective-permute-done.2 = s32[2]{0:T(128)S(1)} collective-permute-done((s32[2]{0:T(128)S(1)}, s32[2]{0:T(128)S(1)}, u32[]{:S(2)}, u32[]{:S(2)}) %collective-permute-start.2) | collective-permute-done | bytes 40 | tf_op jit(solution)/shard_map/ppermute | solution.py:11
  177.6 3.6 fusion.22
  181.2 3.1 fusion.18
  187.1 33.4 %collective-permute-start.1 = (bf16[2,128,1024]{1,2,0:T(8,128)(2,1)}, bf16[2,128,1024]{1,2,0:T(8,128)(2,1)}, u32[]{:S(2)}, u32[]{:S(2)}) collective-permute-start(bf16[2,128,1024]{1,2,0:T(8,128)(2,1)} %get-tuple-element.50), channel_id=1, source_target_pairs={{0,128},{8,136},{16,144},{24,152},{32,160},{40,168},{48,176},{56,1... | collective-permute-start | bytes 1572872 | tf_op jit(solution)/shard_map/ppermute | solution.py:11
  222.2 6.4 %all-to-all-start.2 = ((s32[128,8,1]{0,2,1:T(1,128)}), s32[128,8,1]{0,2,1:T(1,128)S(1)}, u32[]{:S(2)}, u32[]{:S(2)}) async-start(s32[128,8,1]{0,2,1:T(1,128)} %broadcast_in_dim.186), calls=%async_computation.2 | async-start | bytes 8192 | tf_op jit(solution)/shard_map/all_to_all | solution.py:86
  228.6 10.4 %collective-permute-done.1 = bf16[2,128,1024]{1,2,0:T(8,128)(2,1)} collective-permute-done((bf16[2,128,1024]{1,2,0:T(8,128)(2,1)}, bf16[2,128,1024]{1,2,0:T(8,128)(2,1)}, u32[]{:S(2)}, u32[]{:S(2)}) %collective-permute-start.1) | collective-permute-done | bytes 524320 | tf_op jit(solution)/shard_map/ppermute | solution.py:11
  239.1 23.1 %collective-permute-done.4 = bf16[2,128,1024]{1,2,0:T(8,128)(2,1)} collective-permute-done((bf16[2,128,1024]{1,2,0:T(8,128)(2,1)}, bf16[2,128,1024]{1,2,0:T(8,128)(2,1)}, u32[]{:S(2)}, u32[]{:S(2)}) %collective-permute-start.4) | collective-permute-done | bytes 524320 | tf_op jit(solution)/shard_map/ppermute | solution.py:11
  265.0 9.8 %all-to-all-start.1 = ((s32[128,8,1]{0,2,1:T(1,128)}), s32[128,8,1]{0,2,1:T(1,128)S(1)}, u32[]{:S(2)}, u32[]{:S(2)}) async-start(s32[128,8,1]{0,2,1:T(1,128)} %broadcast_in_dim.185), calls=%async_computation.1 | async-start | bytes 8192 | tf_op jit(solution)/shard_map/all_to_all | solution.py:85
  274.8 3.1 fusion.30
  279.4 4.2 all-to-all-start
  283.5 4.2 fusion.15
  290.1 4.7 all-to-all-start.3
  295.9 13.9 %all-to-all-done.3 = bf16[128,8,512]{0,2,1:T(8,128)(2,1)S(1)} async-done(((bf16[128,8,512]{0,2,1:T(8,128)(2,1)}), bf16[128,8,512]{0,2,1:T(8,128)(2,1)S(1)}, u32[]{:S(2)}, u32[]{:S(2)}) %all-to-all-start.3) | async-done | bytes 1048608 | tf_op jit(solution)/shard_map/all_to_all | solution.py:82
  309.8 4.8 all-to-all-start.4
  316.2 10.1 %convolution_convert_fusion.1 = bf16[1024,512]{1,0:T(8,128)(2,1)} fusion(bf16[1024,4096]{1,0:T(8,128)(2,1)} %all-gather.2.cloned.1.call-done, bf16[512,4096]{1,0:T(8,128)(2,1)} %param.12), kind=kOutput, calls=%fused_computation.23 | convolution fusion | flops 4295491584 | bytes 13631488 | tf_op jit(solution)/shard_map/dot_general | solution.py:105
  326.3 2.7 reshape.204
  329.0 3.0 copy.61
  332.0 3.2 multiply_reduce_fusion
  335.9 9.5 %convolution_convert_fusion = bf16[512,4096]{1,0:T(8,128)(2,1)} fusion(bf16[1024,4096]{1,0:T(8,128)(2,1)} %all-gather.2.cloned.1.call-done, bf16[64,8,8,128]{3,2,1,0:T(8,128)(2,1)S(1)} %bitcast.249), kind=kOutput, calls=%fused_computation | convolution fusion | flops 4297064448 | bytes 13631488 | tf_op jit(solution)/shard_map/dot_general | solution.py:108
  345.4 6.5 %copy.87 = bf16[512,4096]{0,1:T(8,128)(2,1)} copy(bf16[512,4096]{1,0:T(8,128)(2,1)} %convolution_convert_fusion) | data formatting | bytes 8388608
  360.5 4.8 all-to-all-start.6
  365.4 2.8 fusion.13
  368.2 3.8 all-to-all-done.6
  372.0 4.4 all-to-all-start.7
  377.8 5.1 all-to-all-done.7
  382.8 4.5 all-to-all-start.5
  390.0 12.5 %all-to-all-done.5 = bf16[8,128,512]{1,2,0:T(8,128)(2,1)S(1)} async-done(((bf16[8,128,512]{1,2,0:T(8,128)(2,1)}), bf16[8,128,512]{1,2,0:T(8,128)(2,1)S(1)}, u32[]{:S(2)}, u32[]{:S(2)}) %all-to-all-start.5) | async-done | bytes 1048608 | tf_op jit(solution)/shard_map/all_to_all | solution.py:135
  403.8 165.3 %reduce-scatter.4.cloned.1.call-done = bf16[128,512]{1,0:T(8,128)(2,1)} async-done(((bf16[4096,512]{1,0:T(8,128)(2,1)}), bf16[128,512]{1,0:T(8,128)(2,1)}) %reduce-scatter.4.cloned.1.call-update) | async-done | bytes 131088
  (69 shorter events, 33.3 us)
Async XLA Ops:
  7.2 309.1 %all-gather.2.cloned.1.call-start = ((), (), s32[]{:S(2)}) async-start(), calls=%async_computation.9 | async-start | bytes 9437184 | tf_op jit(solution)/shard_map/all_gather | solution.py:104
  8.6 17.9 %copy-start.8 = (s32[2]{0:T(128)S(1)}, s32[2]{0:T(128)}, u32[]{:S(2)}) copy-start(s32[2]{0:T(128)} %param.15) | copy-start | bytes 28
  8.6 21.1 %copy-start = (bf16[2,128,4096]{2,1,0:T(8,128)(2,1)S(1)}, bf16[2,128,4096]{2,1,0:T(8,128)(2,1)}, u32[]{:S(2)}) copy-start(bf16[2,128,4096]{2,1,0:T(8,128)(2,1)} %param.11) | copy-start | bytes 6291460
  13.4 164.2 %collective-permute-start.3 = (bf16[2,128,4096]{2,1,0:T(8,128)(2,1)}, bf16[2,128,4096]{2,1,0:T(8,128)(2,1)}, u32[]{:S(2)}, u32[]{:S(2)}) collective-permute-start(bf16[2,128,4096]{2,1,0:T(8,128)(2,1)} %get-tuple-element.52), channel_id=1, source_target_pairs={{0,128},{8,136},{16,144},{24,152},{32,160},{40,168},{48,176},{56,1... | collective-permute-start | bytes 6291464 | tf_op jit(solution)/shard_map/ppermute | solution.py:11
  21.1 156.4 %collective-permute-start.5 = (bf16[2,128,4096]{2,1,0:T(8,128)(2,1)}, bf16[2,128,4096]{2,1,0:T(8,128)(2,1)}, u32[]{:S(2)}, u32[]{:S(2)}) collective-permute-start(bf16[2,128,4096]{2,1,0:T(8,128)(2,1)} %get-tuple-element.53), channel_id=1, source_target_pairs={{0,128},{8,136},{16,144},{24,152},{32,160},{40,168},{48,176},{56,1... | collective-permute-start | bytes 6291464 | tf_op jit(solution)/shard_map/ppermute | solution.py:11
  21.2 156.3 %collective-permute-start = (s32[2]{0:T(128)S(1)}, s32[2]{0:T(128)S(1)}, u32[]{:S(2)}, u32[]{:S(2)}) collective-permute-start(s32[2]{0:T(128)S(1)} %get-tuple-element.16), channel_id=1, source_target_pairs={{0,128},{8,136},{16,144},{24,152},{32,160},{40,168},{48,176},{56,1... | collective-permute-start | bytes 32 | tf_op jit(solution)/shard_map/ppermute | solution.py:11
  26.5 147.8 %collective-permute-start.2 = (s32[2]{0:T(128)S(1)}, s32[2]{0:T(128)S(1)}, u32[]{:S(2)}, u32[]{:S(2)}) collective-permute-start(s32[2]{0:T(128)S(1)} %copy-done.8), channel_id=1, source_target_pairs={{0,128},{8,136},{16,144},{24,152},{32,160},{40,168},{48,176},{56,1... | collective-permute-start | bytes 32 | tf_op jit(solution)/shard_map/ppermute | solution.py:11
  177.6 3.7 copy-start.2
  177.6 3.7 copy-start.3
  181.2 3.1 copy-start.7
  187.1 52.0 %collective-permute-start.1 = (bf16[2,128,1024]{1,2,0:T(8,128)(2,1)}, bf16[2,128,1024]{1,2,0:T(8,128)(2,1)}, u32[]{:S(2)}, u32[]{:S(2)}) collective-permute-start(bf16[2,128,1024]{1,2,0:T(8,128)(2,1)} %get-tuple-element.50), channel_id=1, source_target_pairs={{0,128},{8,136},{16,144},{24,152},{32,160},{40,168},{48,176},{56,1... | collective-permute-start | bytes 1572872 | tf_op jit(solution)/shard_map/ppermute | solution.py:11
  220.4 41.7 %collective-permute-start.4 = (bf16[2,128,1024]{1,2,0:T(8,128)(2,1)}, bf16[2,128,1024]{1,2,0:T(8,128)(2,1)}, u32[]{:S(2)}, u32[]{:S(2)}) collective-permute-start(bf16[2,128,1024]{1,2,0:T(8,128)(2,1)} %get-tuple-element.51), channel_id=1, source_target_pairs={{0,128},{8,136},{16,144},{24,152},{32,160},{40,168},{48,176},{56,1... | collective-permute-start | bytes 1572872 | tf_op jit(solution)/shard_map/ppermute | solution.py:11
  222.2 42.2 %all-to-all-start.2 = ((s32[128,8,1]{0,2,1:T(1,128)}), s32[128,8,1]{0,2,1:T(1,128)S(1)}, u32[]{:S(2)}, u32[]{:S(2)}) async-start(s32[128,8,1]{0,2,1:T(1,128)} %broadcast_in_dim.186), calls=%async_computation.2 | async-start | bytes 8192 | tf_op jit(solution)/shard_map/all_to_all | solution.py:86
  264.4 19.2 %copy-start.1 = (bf16[128,4096]{1,0:T(8,128)(2,1)S(1)}, bf16[128,4096]{1,0:T(8,128)(2,1)}, u32[]{:S(2)}) copy-start(bf16[128,4096]{1,0:T(8,128)(2,1)} %get-tuple-element.39) | copy-start | bytes 3145732
  265.0 14.4 %all-to-all-start.1 = ((s32[128,8,1]{0,2,1:T(1,128)}), s32[128,8,1]{0,2,1:T(1,128)S(1)}, u32[]{:S(2)}, u32[]{:S(2)}) async-start(s32[128,8,1]{0,2,1:T(1,128)} %broadcast_in_dim.185), calls=%async_computation.1 | async-start | bytes 8192 | tf_op jit(solution)/shard_map/all_to_all | solution.py:85
  279.4 10.7 %all-to-all-start = ((bf16[128,8,128]{2,0,1:T(8,128)(2,1)}), bf16[128,8,128]{2,0,1:T(8,128)(2,1)S(1)}, u32[]{:S(2)}, u32[]{:S(2)}) async-start(bf16[128,8,128]{2,0,1:T(8,128)(2,1)} %copy.51), calls=%async_computation | async-start | bytes 524288 | tf_op jit(solution)/shard_map/all_to_all | solution.py:83
  287.7 7.3 %copy-start.6 = (bf16[128,1024]{0,1:T(8,128)(2,1)S(1)}, bf16[128,1024]{0,1:T(8,128)(2,1)}, u32[]{:S(2)}) copy-start(bf16[128,1024]{0,1:T(8,128)(2,1)} %get-tuple-element.69) | copy-start | bytes 786436
  290.1 19.8 %all-to-all-start.3 = ((bf16[128,8,512]{0,2,1:T(8,128)(2,1)}), bf16[128,8,512]{0,2,1:T(8,128)(2,1)S(1)}, u32[]{:S(2)}, u32[]{:S(2)}) async-start(bf16[128,8,512]{0,2,1:T(8,128)(2,1)} %bitcast.31), calls=%async_computation.3 | async-start | bytes 2097152 | tf_op jit(solution)/shard_map/all_to_all | solution.py:82
  309.8 22.1 %all-to-all-start.4 = ((bf16[128,8,128]{2,0,1:T(8,128)(2,1)}), bf16[128,8,128]{2,0,1:T(8,128)(2,1)}, u32[]{:S(2)}, u32[]{:S(2)}) async-start(bf16[128,8,128]{2,0,1:T(8,128)(2,1)} %copy.57), calls=%async_computation.4 | async-start | bytes 524288 | tf_op jit(solution)/shard_map/all_to_all | solution.py:84
  314.6 254.4 %reduce-scatter.4.cloned.1.call-start = ((), (), s32[]{:S(2)}) async-start(), calls=%async_computation.10 | async-start | bytes 4325376
  358.4 1.0 copy-start.4
  360.5 11.4 %all-to-all-start.6 = ((bf16[8,128,128]{1,2,0:T(8,128)(2,1)}), bf16[8,128,128]{1,2,0:T(8,128)(2,1)}, u32[]{:S(2)}, u32[]{:S(2)}) async-start(bf16[8,128,128]{1,2,0:T(8,128)(2,1)} %fusion.12), calls=%async_computation.6 | async-start | bytes 524288 | tf_op jit(solution)/shard_map/all_to_all | solution.py:136
  365.4 11.0 %copy-start.5 = (bf16[8,4,128,128]{2,3,1,0:T(8,128)(2,1)S(1)}, bf16[8,4,128,128]{2,3,1,0:T(8,128)(2,1)}, u32[]{:S(2)}) copy-start(bf16[8,4,128,128]{2,3,1,0:T(8,128)(2,1)} %copy-done.4) | copy-start | bytes 3145732
  372.0 10.9 %all-to-all-start.7 = ((bf16[8,128,128]{1,2,0:T(8,128)(2,1)}), bf16[8,128,128]{1,2,0:T(8,128)(2,1)S(1)}, u32[]{:S(2)}, u32[]{:S(2)}) async-start(bf16[8,128,128]{1,2,0:T(8,128)(2,1)} %fusion.13), calls=%async_computation.7 | async-start | bytes 524288 | tf_op jit(solution)/shard_map/all_to_all | solution.py:137
  382.8 19.6 %all-to-all-start.5 = ((bf16[8,128,512]{1,2,0:T(8,128)(2,1)}), bf16[8,128,512]{1,2,0:T(8,128)(2,1)S(1)}, u32[]{:S(2)}, u32[]{:S(2)}) async-start(bf16[8,128,512]{1,2,0:T(8,128)(2,1)} %bitcast.61), calls=%async_computation.5 | async-start | bytes 2097152 | tf_op jit(solution)/shard_map/all_to_all | solution.py:135
Sparse Core Ops, SparseCore 0:
  184.5 83.1 all-gather.1
  352.0 217.0 reduce-scatter.3
where the time goes:
time: 583 us; the launch traced here: 578 us
  waiting for transfers between devices  376 us (64%)
  starting transfers between devices  90.1 us (15%)
  local copies, waits for them, and re-layouts  31.3 us (5%)
  matrix products  30.7 us (5%)
  other arithmetic  30.3 us (5%)
  between operations  19.4 us (3%)
    ppermute x6, waiting for transfers between devices, passed_along(): lax.ppermute(array, axis, [(i, (i + by) % devices) for i in range(devices)])  175 us
    unnamed x3, waiting for transfers between devices  165 us
    ppermute x6, starting transfers between devices, passed_along(): lax.ppermute(array, axis, [(i, (i + by) % devices) for i in range(devices)])  46.6 us
    all_to_all x1, waiting for transfers between devices, local(): lax.all_to_all(dest_fields[0], 'tensor', split_axis=1, concat_axis=0, til...  13.9 us
    unnamed x24, local copies, waits for them, and re-layouts  12.7 us
    all_to_all x1, waiting for transfers between devices, local(): lax.all_to_all(query_heads, 'tensor', split_axis=0, concat_axis=1, tiled=...  12.5 us
  transfers between devices with their start and end apart: 16, of which 9 were waited for; matrix products, arithmetic and copies ran while one was open for 10% of the time, Pallas kernels for 0%

commit v1 on v0

v1 whole, which is shorter than its diff:
```python
import functools

import jax
import jax.numpy as jnp
from jax import lax
from jax.experimental import pallas as pl
from jax.experimental.pallas import tpu as pltpu
from jax.sharding import PartitionSpec as P

MESH = pl.DeviceIdType.MESH
BF = jnp.bfloat16
F32 = jnp.float32
HD = 128
T = 128
X = 4
Z = 8
NT = 8
KV = 8
GROUP = 4
NN = (((1,), (0,)), ((), ()))
NTD = (((1,), (1,)), ((), ()))
TN = (((0,), (0,)), ((), ()))


def dot(a, b, dims=NN):
    return lax.dot_general(a, b, dims, preferred_element_type=F32)


def tile(index, size=128):
    start = index * size
    if not isinstance(index, int):
        start = pl.multiple_of(start, size)
    return pl.ds(start, size)


def kernel(
    q_hbm, k_hbm, v_hbm, g_hbm, w_hbm, len_ref, grp_ref, off_ref,
    qg_ref, kg_ref, vg_ref, wg_ref,
    xin, wv, pack, mask, lab_s, lab_r,
    send, keep, got, gall,
    ag_s, ag_r, at_s, at_r, probs, outs, dk, dv,
    xs, xr, zs, zr,
    in_sem, zsend, zrecv, lsem, ysend, yrecv, csend, crecv,
    agsend, agrecv, atsend, atrecv, xsend, xrecv, rsend, rrecv,
):
    dp = lax.axis_index("dp")
    t = lax.axis_index("tensor")
    z = dp // X
    x = dp % X

    def at_z(d):
        return (lax.rem(z + d, Z) * X + x, t)

    def at_x(d):
        return (z * X + lax.rem(x + d, X), t)

    def at_t(d):
        return (dp, lax.rem(t + d, NT))

    partner = at_z(Z // 2)
    sibling_t = t + 1 - 2 * lax.rem(t, 2)
    sibling = (dp, sibling_t)

    def rcopy(src, dst, ssem, rsem, device):
        return pltpu.make_async_remote_copy(
            src_ref=src, dst_ref=dst, send_sem=ssem, recv_sem=rsem,
            device_id=device, device_id_type=MESH,
        )

    barrier = pltpu.get_barrier_semaphore()
    peers = [at_z(d) for d in range(1, Z)] + [at_x(d) for d in range(1, X)]
    peers = peers + [at_t(d) for d in range(1, NT)]
    for peer in peers:
        pl.semaphore_signal(barrier, inc=1, device_id=peer, device_id_type=MESH)

    loads = []
    for hbm, start, width in ((g_hbm, 0, 4096), (k_hbm, 4096, 1024), (v_hbm, 5120, 1024), (q_hbm, 6144, 4096)):
        for slot in range(2):
            loads.append(
                pltpu.make_async_copy(
                    hbm.at[slot],
                    xin.at[slot * T : (slot + 1) * T, start : start + width],
                    in_sem.at[len(loads)],
                )
            )
    loads.append(pltpu.make_async_copy(w_hbm, wv, in_sem.at[len(loads)]))
    for load in loads:
        load.start()

    rows = lax.broadcasted_iota(jnp.int32, (T, T), 0)
    cols = lax.broadcasted_iota(jnp.int32, (T, T), 1)
    moved_off = jnp.int32(0)
    kept_off = jnp.int32(0)
    for slot in range(2):
        length = len_ref[slot]
        offset = off_ref[slot]
        moving = jnp.where(grp_ref[slot] != dp, 1, 0)
        hit = jnp.where((cols < length) & (rows == cols + offset), 1.0, 0.0)
        went = moving.astype(F32)
        pack[0:T, slot * T : (slot + 1) * T] = (hit * went).astype(BF)
        pack[T : 2 * T, slot * T : (slot + 1) * T] = (hit * (1.0 - went)).astype(BF)
        moved_off = moved_off + moving * offset
        kept_off = kept_off + (1 - moving) * offset
    lab_s[...] = jnp.zeros((8, 128), jnp.int32) + moved_off

    def zcopy(i):
        return rcopy(send.at[i], got.at[i], zsend.at[i], zrecv.at[i], partner)

    label_copy = rcopy(lab_s, lab_r, lsem.at[0], lsem.at[1], partner)

    def packed(start):
        return dot(pack[...], xin[:, pl.ds(pl.multiple_of(start, 512), 512)])

    loads[0].wait()
    loads[1].wait()
    own_rows = tile(t)
    for i in range(4):
        for half in range(2):
            both = packed(i * 1024 + half * 512).astype(BF)
            send[i, :, half * 512 : (half + 1) * 512] = both[0:T]
            gall[own_rows, i * 1024 + half * 512 : i * 1024 + (half + 1) * 512] = both[T:]
        if i == 0:
            pl.semaphore_wait(barrier, len(peers))
            label_copy.start()
            zcopy(0).start()
        if i == 1:
            zcopy(1).start()
    for load in loads[2:8]:
        load.wait()
    for i in range(2):
        for half in range(2):
            both = packed(4096 + i * 1024 + half * 512).astype(BF)
            send[4 + i, :, half * 512 : (half + 1) * 512] = both[0:T]
            keep[i, :, half * 512 : (half + 1) * 512] = both[T:]

    def pack_q(c, carry):
        both = packed(6144 + c * 512).astype(BF)
        for j in range(GROUP):
            part = both[:, j * HD : (j + 1) * HD]
            send[6 + j, :, tile(c)] = part[0:T]
            keep[2 + j, :, tile(c)] = part[T:]
        return carry

    lax.fori_loop(0, KV, pack_q, 0)

    def block(i, row_t):
        return gall.at[tile(row_t), i * 1024 : (i + 1) * 1024]

    def ycopy(i, n, row_t):
        return rcopy(block(i, row_t), block(i, row_t), ysend.at[i, n], yrecv.at[i, n], at_t(2 * (n + 1)))

    def ccopy(i, n, row_t):
        return rcopy(block(i, row_t), block(i, row_t), csend.at[i, n], crecv.at[i, n], sibling)

    def from_t(n):
        return lax.rem(t + NT - 2 * (n + 1), NT)

    def sib_from_t(n):
        return lax.rem(sibling_t + NT - 2 * (n + 1), NT)

    def forward(i):
        for n in (0, 2, 1):
            ycopy(i, n, from_t(n)).wait_recv()
            ccopy(i, n, from_t(n)).start()

    for i in range(4):
        zcopy(i).wait_recv()
        zcopy(i + 2).start()
        lanes = slice(i * 1024, (i + 1) * 1024)
        gall[own_rows, lanes] = gall[own_rows, lanes] + got[i]
        for n in (1, 0, 2):
            ycopy(i, n, t).start()
        ccopy(i, 3, t).start()
        if i > 0:
            forward(i - 1)
    forward(3)
    loads[8].wait()
    for i in range(4):
        for n in range(3):
            ccopy(i, n, sib_from_t(n)).wait_recv()
        ccopy(i, 3, sibling_t).wait_recv()

    def ag_copy(d):
        peer = lax.rem(t + d, NT)
        return rcopy(
            ag_s.at[tile(peer), :], ag_r.at[:, tile(t, 512)],
            agsend.at[d - 1], agrecv.at[d - 1], at_t(d),
        )

    def ag_got(d):
        source = lax.rem(t + NT - d, NT)
        return rcopy(
            ag_s.at[tile(source), :], ag_r.at[:, tile(source, 512)],
            agsend.at[d - 1], agrecv.at[d - 1], at_t(d),
        )

    def ag_block(peer):
        return dot(gall[tile(peer), :], wv[...], NTD).astype(BF)

    def ag_step(d, carry):
        peer = lax.rem(t + d, NT)
        ag_s[tile(peer), :] = ag_block(peer)
        ag_copy(d).start()
        return carry

    lax.fori_loop(1, NT, ag_step, 0)
    ag_r[:, tile(t, 512)] = ag_block(t)

    zcopy(4).wait_recv()
    zcopy(6).start()
    zcopy(5).wait_recv()
    zcopy(7).start()
    label_copy.wait_recv()
    for i in range(2):
        keep[i] = keep[i] + got[4 + i]
    border = lab_r[0:1, :] + kept_off
    crossing = (rows >= border) & (cols < border)
    mask[...] = jnp.where((cols <= rows) & jnp.logical_not(crossing), 1.0, 0.0)
    dk[...] = jnp.zeros_like(dk)
    dv[...] = jnp.zeros_like(dv)
    scale = float(HD) ** (-0.5)

    def at_copy(j, d):
        peer = lax.rem(t + d, NT)
        return rcopy(
            at_s.at[j, peer], at_r.at[j, :, tile(t)],
            atsend.at[j, d - 1], atrecv.at[j, d - 1], at_t(d),
        )

    def at_got(j, d):
        source = lax.rem(t + NT - d, NT)
        return rcopy(
            at_s.at[j, source], at_r.at[j, :, tile(source)],
            atsend.at[j, d - 1], atrecv.at[j, d - 1], at_t(d),
        )

    def xcopy(j, d):
        return rcopy(
            xs.at[j, lax.rem(x + d, X)], xr.at[j, d - 1],
            xsend.at[j, d - 1], xrecv.at[j, d - 1], at_x(d),
        )

    def rcopy_z(j, d):
        return rcopy(
            zs.at[j, lax.rem(z + d, Z)], zr.at[j, d - 1],
            rsend.at[j, d - 1], rrecv.at[j, d - 1], at_z(d),
        )

    def forward_heads(j):
        def step(c, carry):
            query = keep[2 + j, :, tile(c)]
            key = keep[0, :, tile(c)]
            value = keep[1, :, tile(c)]
            allowed = mask[...] > 0.5
            score = jnp.where(allowed, dot(query, key, NTD) * scale, -1e30)
            top = jnp.max(score, axis=-1, keepdims=True)
            expo = jnp.where(allowed, jnp.exp(score - top), 0.0)
            prob = expo / jnp.sum(expo, axis=-1, keepdims=True)
            probs[c] = prob
            out = dot(prob.astype(BF), value)
            outs[c] = out.astype(BF)
            at_s[j, c] = out.T.astype(BF)
            return carry

        lax.fori_loop(0, KV, step, 0, unroll=2)

    def backward_heads(j):
        def step(c, carry):
            query = keep[2 + j, :, tile(c)]
            key = keep[0, :, tile(c)]
            value = keep[1, :, tile(c)]
            grad = ag_r[:, tile(c * GROUP + j)]
            prob = probs[c]
            delta = jnp.sum(grad.astype(F32) * outs[c].astype(F32), axis=-1, keepdims=True)
            score_grad = (prob * (dot(grad, value, NTD) - delta)).astype(BF)
            qg_ref[:, tile(c * GROUP + j)] = (dot(score_grad, key) * scale).astype(BF)
            dk[c] += dot(score_grad, query, TN)
            dv[c] += dot(prob.astype(BF), grad, TN)
            return carry

        lax.fori_loop(0, KV, step, 0, unroll=2)

    def reduce_x(j):
        for d in range(1, X):
            xcopy(j, d).wait_recv()

        def step(zz, carry):
            total = xs[j, x, :, tile(zz)].astype(F32)
            for d in range(1, X):
                total = total + xr[j, d - 1, :, tile(zz)].astype(F32)
            zs[j, zz] = total.astype(BF)
            return carry

        lax.fori_loop(0, Z, step, 0)
        for d in (4, 3, 5, 2, 6, 1, 7):
            rcopy_z(j, d).start()

    def reduce_z(j):
        total = zs[j, z].astype(F32)
        for d in range(1, Z):
            rcopy_z(j, d).wait_recv()
            total = total + zr[j, d - 1].astype(F32)
        wg_ref[j * HD : (j + 1) * HD, :] = total

    for j in range(GROUP):
        zcopy(6 + j).wait_recv()
        if j < 2:
            zcopy(8 + j).start()
        keep[2 + j] = keep[2 + j] + got[6 + j]
        forward_heads(j)
        for d in (4, 3, 5, 2, 6, 1, 7):
            at_copy(j, d).start()
        at_r[j, :, tile(t)] = at_s[j, t]
        if j > 0:
            reduce_x(j - 1)
        for d in range(1, NT):
            at_got(j, d).wait_recv()

        def weight_step(zz, carry):
            term = dot(at_r[j], gall[:, tile(zz, 512)]).astype(BF)
            for xx in range(X):
                xs[j, xx, :, tile(zz)] = term[:, xx * HD : (xx + 1) * HD]
            return carry

        lax.fori_loop(0, Z, weight_step, 0)
        for d in (2, 1, 3):
            xcopy(j, d).start()
        if j == 0:
            for d in range(1, NT):
                ag_got(d).wait_recv()
        backward_heads(j)

    for c in range(KV):
        kg_ref[:, c * HD : (c + 1) * HD] = (dk[c] * scale).astype(BF)
        vg_ref[:, c * HD : (c + 1) * HD] = dv[c].astype(BF)
    for j in range(GROUP - 1):
        reduce_z(j)
    reduce_x(GROUP - 1)

    label_copy.wait_send()
    for i in range(10):
        zcopy(i).wait_send()
    for i in range(4):
        for n in range(3):
            ycopy(i, n, t).wait_send()
            ccopy(i, n, from_t(n)).wait_send()
        ccopy(i, 3, t).wait_send()
    for d in range(1, NT):
        ag_copy(d).wait_send()
    for j in range(GROUP):
        for d in range(1, NT):
            at_copy(j, d).wait_send()
        for d in range(1, X):
            xcopy(j, d).wait_send()
    reduce_z(GROUP - 1)
    for j in range(GROUP):
        for d in range(1, Z):
            rcopy_z(j, d).wait_send()


def local(queries, keys, values, out_grad, out_weight, lengths, dest_group, dest_offset):
    dma = pltpu.SemaphoreType.DMA
    vm = pltpu.VMEM
    return pl.pallas_call(
        kernel,
        out_shape=(
            jax.ShapeDtypeStruct((T, 4096), BF),
            jax.ShapeDtypeStruct((T, 1024), BF),
            jax.ShapeDtypeStruct((T, 1024), BF),
            jax.ShapeDtypeStruct((512, 128), F32),
        ),
        in_specs=[pl.BlockSpec(memory_space=pl.ANY)] * 5 + [pl.BlockSpec(memory_space=pltpu.SMEM)] * 3,
        out_specs=tuple([pl.BlockSpec(memory_space=pltpu.VMEM)] * 4),
        scratch_shapes=[
            vm((2 * T, 10240), BF),
            vm((512, 4096), BF),
            vm((2 * T, 2 * T), BF),
            vm((T, T), F32),
            vm((8, 128), jnp.int32),
            vm((8, 128), jnp.int32),
            vm((10, T, 1024), BF),
            vm((6, T, 1024), BF),
            vm((10, T, 1024), BF),
            vm((NT * T, 4096), BF),
            vm((NT * T, 512), BF),
            vm((T, 4096), BF),
            vm((GROUP, KV, HD, T), BF),
            vm((GROUP, HD, NT * T), BF),
            vm((KV, T, T), F32),
            vm((KV, T, HD), BF),
            vm((KV, T, HD), F32),
            vm((KV, T, HD), F32),
            vm((GROUP, X, HD, 1024), BF),
            vm((GROUP, X - 1, HD, 1024), BF),
            vm((GROUP, Z, HD, 128), BF),
            vm((GROUP, Z - 1, HD, 128), BF),
            dma((9,)),
            dma((10,)), dma((10,)),
            dma((2,)),
            dma((4, 3)), dma((4, 3)),
            dma((4, 4)), dma((4, 4)),
            dma((7,)), dma((7,)),
            dma((4, 7)), dma((4, 7)),
            dma((4, 3)), dma((4, 3)),
            dma((4, 7)), dma((4, 7)),
        ],
        compiler_params=pltpu.CompilerParams(
            collective_id=0, has_side_effects=True, vmem_limit_bytes=60 * 2**20
        ),
        cost_estimate=pl.CostEstimate(flops=30_000_000_000, bytes_accessed=12_000_000, transcendentals=600_000),
    )(queries, keys, values, out_grad, out_weight, lengths, dest_group, dest_offset)


def solution(mesh):
    in_specs = (
        P(("dp", "tensor"), None, None),
        P(("dp", "tensor"), None, None),
        P(("dp", "tensor"), None, None),
        P(("dp", "tensor"), None, None),
        P("tensor", None),
        P(("dp", "tensor")),
        P(("dp", "tensor")),
        P(("dp", "tensor")),
    )
    out_specs = (
        P(("dp", "tensor"), None),
        P(("dp", "tensor"), None),
        P(("dp", "tensor"), None),
        P("tensor", "dp"),
    )
    return jax.shard_map(local, mesh=mesh, in_specs=in_specs, out_specs=out_specs, check_vma=False)
```

time: 583 us -> 200 us (0.34)
  waiting for transfers between devices: 376 us -> 0 us
  Pallas kernels: 0 us -> 194 us
  starting transfers between devices: 90.1 us -> 0 us
  matrix products: 30.7 us -> 0 us
  other arithmetic: 30.3 us -> 0 us
  local copies, waits for them, and re-layouts: 31.3 us -> 4.48 us
  between operations: 19.4 us -> 0.67 us
    pallas_call x0 -> x1, Pallas kernels: none -> 194 us  [local(): pl.pallas_call(kernel, out_shape=(jax.ShapeDtypeStruct((T, 4096), BF), ja...]
    ppermute x6 -> x0, waiting for transfers between devices: 175 us -> none  [passed_along(): lax.ppermute(array, axis, [(i, (i + by) % devices) for i in range(devices)])]
    unnamed x3 -> x0, waiting for transfers between devices: 165 us -> none
    ppermute x6 -> x0, starting transfers between devices: 46.6 us -> none  [passed_along(): lax.ppermute(array, axis, [(i, (i + by) % devices) for i in range(devices)])]
    all_to_all x8 -> x0, starting transfers between devices: 43.5 us -> none  [the longest x1 9.83 us: local(): lax.all_to_all(label_wide, 'tensor', split_axis=1, concat_axis=0, tiled=T...]
    all_to_all x8 -> x0, waiting for transfers between devices: 35.9 us -> none  [the longest x1 13.9 us: local(): lax.all_to_all(dest_fields[0], 'tensor', split_axis=1, concat_axis=0, til...]
    dot_general x8 -> x0, matrix products: 30.7 us -> none  [the longest x1 10.1 us: local(): lax.dot_general(piece, out_weight, (((1,), (1,)), ((), ())), preferred_el...]
    select_n x9 -> x0, other arithmetic: 16.8 us -> none  [the longest x4 10.2 us: pack_rows(): jnp.where(mask[member][:, None], field[member], jnp.zeros_like(field[memb...]
  transfers between devices with their start and end apart: 16 -> 0, of which waited for: 9 -> 0; matrix products, arithmetic and copies ran while one was open for 10% -> 0% of each run, Pallas kernels for 0% -> 0%
where the time goes in v1:
time: 200 us; the launch traced here: 199 us
  Pallas kernels  194 us (97%)
  local copies, waits for them, and re-layouts  4.48 us (2%)
    pallas_call x1, Pallas kernels, local(): pl.pallas_call(kernel, out_shape=(jax.ShapeDtypeStruct((T, 4096), BF), ja...  194 us
    unnamed x10, local copies, waits for them, and re-layouts  4.48 us

profile of v1, /device:TPU:1, one launch (start us, length us, event | category | flops | bytes accessed | tf_op | source)
XLA Modules:
  0.0 198.8 jit_solution(13720193476752776265)
XLA Ops:
  0.6 193.6 %shard_map.111 = (bf16[128,4096]{1,0:T(8,128)(2,1)}, bf16[128,1024]{1,0:T(8,128)(2,1)}, bf16[128,1024]{1,0:T(8,128)(2,1)}, f32[512,128]{1,0:T(8,128)}) custom-call(bf16[2,128,4096]{2,1,0:T(8,128)(2,1)} %q_hbm.1, bf16[2,128,1024]{2,1,0:T(8,128)(2,1)} %k_hbm.1, bf16[2,128,1024]{2,1,0:T(8,128)(2,1)} %v_hbm.1, bf16[2,128,4096]{2,1,0:T(8,128)(2,1)} %g_hbm.1, ...), custom_call_target="tpu_custom_call" | custom-call | flops 30000001024 | bytes 12000000 | tf_op jit(solution)/shard_map/pallas_call | solution.py:364
  194.3 0.0 copy-start.2
  194.3 0.0 copy-start.1
  194.3 0.0 copy-start
  194.3 2.4 %copy.16 = bf16[128,4096]{1,0:T(8,128)(2,1)} copy(bf16[128,4096]{1,0:T(8,128)(2,1)} %get-tuple-element.8) | data formatting | bytes 2097152
  196.7 0.0 copy-done.2
  196.7 0.7 copy.17
  197.4 0.0 copy-done.1
  197.4 0.7 copy.18
  198.1 0.0 copy-done
  198.1 0.7 copy.19
Async XLA Ops:
  194.3 2.4 %copy-start.2 = (bf16[128,1024]{1,0:T(8,128)(2,1)S(1)}, bf16[128,1024]{1,0:T(8,128)(2,1)}, u32[]{:S(2)}) copy-start(bf16[128,1024]{1,0:T(8,128)(2,1)} %get-tuple-element.9) | copy-start | bytes 786436
  194.3 3.1 %copy-start.1 = (bf16[128,1024]{1,0:T(8,128)(2,1)S(1)}, bf16[128,1024]{1,0:T(8,128)(2,1)}, u32[]{:S(2)}) copy-start(bf16[128,1024]{1,0:T(8,128)(2,1)} %get-tuple-element.10) | copy-start | bytes 786436
  194.3 3.8 %copy-start = (f32[512,128]{1,0:T(8,128)S(1)}, f32[512,128]{1,0:T(8,128)}, u32[]{:S(2)}) copy-start(f32[512,128]{1,0:T(8,128)} %get-tuple-element.11) | copy-start | bytes 786436

commit v2 on v1

--- a/solution.py
+++ b/solution.py
@@ -20,6 +20,7 @@
 NN = (((1,), (0,)), ((), ()))
 NTD = (((1,), (1,)), ((), ()))
 TN = (((0,), (0,)), ((), ()))
+PLACE = {4: 0, 2: 1, 0: 2, 6: 3, 3: 4, 5: 5, 7: 6, 1: 7}
 
 
 def dot(a, b, dims=NN):
@@ -31,6 +32,10 @@
     if not isinstance(index, int):
         start = pl.multiple_of(start, size)
     return pl.ds(start, size)
+
+
+def seat(c):
+    return lax.rem(c, 2) * 4 + c // 2
 
 
 def kernel(
@@ -40,7 +45,7 @@
     send, keep, got, gall,
     ag_s, ag_r, at_s, at_r, probs, outs, dk, dv,
     xs, xr, zs, zr,
-    in_sem, zsend, zrecv, lsem, ysend, yrecv, csend, crecv,
+    in_sem, zsend, zrecv, qsend, qrecv, lsem, ysend, yrecv, csend, crecv,
     agsend, agrecv, atsend, atrecv, xsend, xrecv, rsend, rrecv,
 ):
     dp = lax.axis_index("dp")
@@ -105,6 +110,16 @@
 
     def zcopy(i):
         return rcopy(send.at[i], got.at[i], zsend.at[i], zrecv.at[i], partner)
+
+    def qcopy(j, p):
+        lanes = slice(p * 512, (p + 1) * 512)
+        return rcopy(
+            send.at[6 + j, :, lanes], got.at[6 + j, :, lanes], qsend.at[j, p], qrecv.at[j, p], partner
+        )
+
+    def start_q(j):
+        for p in range(2):
+            qcopy(j, p).start()
 
     label_copy = rcopy(lab_s, lab_r, lsem.at[0], lsem.at[1], partner)
 
@@ -137,8 +152,8 @@
         both = packed(6144 + c * 512).astype(BF)
         for j in range(GROUP):
             part = both[:, j * HD : (j + 1) * HD]
-            send[6 + j, :, tile(c)] = part[0:T]
-            keep[2 + j, :, tile(c)] = part[T:]
+            send[6 + j, :, tile(seat(c))] = part[0:T]
+            keep[2 + j, :, tile(seat(c))] = part[T:]
         return carry
 
     lax.fori_loop(0, KV, pack_q, 0)
@@ -180,6 +195,9 @@
             ccopy(i, n, sib_from_t(n)).wait_recv()
         ccopy(i, 3, sibling_t).wait_recv()
 
+    zcopy(4).wait_recv()
+    start_q(0)
+
     def ag_copy(d):
         peer = lax.rem(t + d, NT)
         return rcopy(
@@ -206,10 +224,8 @@
     lax.fori_loop(1, NT, ag_step, 0)
     ag_r[:, tile(t, 512)] = ag_block(t)
 
-    zcopy(4).wait_recv()
-    zcopy(6).start()
     zcopy(5).wait_recv()
-    zcopy(7).start()
+    start_q(1)
     label_copy.wait_recv()
     for i in range(2):
         keep[i] = keep[i] + got[4 + i]
@@ -234,39 +250,57 @@
             atsend.at[j, d - 1], atrecv.at[j, d - 1], at_t(d),
         )
 
-    def xcopy(j, d):
-        return rcopy(
-            xs.at[j, lax.rem(x + d, X)], xr.at[j, d - 1],
-            xsend.at[j, d - 1], xrecv.at[j, d - 1], at_x(d),
+    def distance(half, k):
+        return lax.rem(4 + 6 * k, Z) if half == 0 else lax.rem(3 + 2 * k, Z)
+
+    def xcopy(j, half, d):
+        lanes = slice(half * 512, (half + 1) * 512)
+        return rcopy(
+            xs.at[j, lax.rem(x + d, X), :, lanes], xr.at[j, d - 1, :, lanes],
+            xsend.at[j, half, d - 1], xrecv.at[j, half, d - 1], at_x(d),
         )
 
     def rcopy_z(j, d):
         return rcopy(
-            zs.at[j, lax.rem(z + d, Z)], zr.at[j, d - 1],
+            zs.at[j, PLACE[d]], zr.at[j, d - 1],
             rsend.at[j, d - 1], rrecv.at[j, d - 1], at_z(d),
         )
 
-    def forward_heads(j):
-        def step(c, carry):
-            query = keep[2 + j, :, tile(c)]
+    def send_attended(j, p):
+        def step(m, carry):
+            peer = 2 * m + p
+
+            @pl.when(peer != t)
+            def _():
+                at_copy(j, lax.rem(peer + NT - t, NT)).start()
+
+            return carry
+
+        lax.fori_loop(0, 4, step, 0)
+
+    def forward_heads(j, p):
+        def step(m, carry):
+            c = 2 * m + p
+            query = keep[2 + j, :, tile(p * 4 + m)]
             key = keep[0, :, tile(c)]
             value = keep[1, :, tile(c)]
             allowed = mask[...] > 0.5
             score = jnp.where(allowed, dot(query, key, NTD) * scale, -1e30)
             top = jnp.max(score, axis=-1, keepdims=True)
-            expo = jnp.where(allowed, jnp.exp(score - top), 0.0)
+            expo = jnp.exp(score - top)
             prob = expo / jnp.sum(expo, axis=-1, keepdims=True)
             probs[c] = prob
             out = dot(prob.astype(BF), value)
-            outs[c] = out.astype(BF)
-            at_s[j, c] = out.T.astype(BF)
+            out = out.astype(BF)
+            outs[c] = out
+            at_s[j, c] = out.T
             return carry
 
-        lax.fori_loop(0, KV, step, 0, unroll=2)
+        lax.fori_loop(0, 4, step, 0, unroll=4)
 
     def backward_heads(j):
         def step(c, carry):
-            query = keep[2 + j, :, tile(c)]
+            query = keep[2 + j, :, tile(seat(c))]
             key = keep[0, :, tile(c)]
             value = keep[1, :, tile(c)]
             grad = ag_r[:, tile(c * GROUP + j)]
@@ -278,68 +312,90 @@
             dv[c] += dot(prob.astype(BF), grad, TN)
             return carry
 
-        lax.fori_loop(0, KV, step, 0, unroll=2)
-
-    def reduce_x(j):
+        lax.fori_loop(0, KV, step, 0, unroll=4)
+
+    def reduce_x(j, half):
         for d in range(1, X):
-            xcopy(j, d).wait_recv()
-
-        def step(zz, carry):
-            total = xs[j, x, :, tile(zz)].astype(F32)
+            xcopy(j, half, d).wait_recv()
+
+        def step(k, carry):
+            place = half * 4 + k
+            total = xs[j, x, :, tile(place)].astype(F32)
             for d in range(1, X):
-                total = total + xr[j, d - 1, :, tile(zz)].astype(F32)
-            zs[j, zz] = total.astype(BF)
+                total = total + xr[j, d - 1, :, tile(place)].astype(F32)
+            zs[j, place] = total.astype(BF)
             return carry
 
-        lax.fori_loop(0, Z, step, 0)
-        for d in (4, 3, 5, 2, 6, 1, 7):
+        lax.fori_loop(0, 4, step, 0)
+
+    def send_z(j, half):
+        for d in ((4, 2, 6), (3, 5, 1, 7))[half]:
             rcopy_z(j, d).start()
 
     def reduce_z(j):
-        total = zs[j, z].astype(F32)
-        for d in range(1, Z):
+        total = zs[j, PLACE[0]].astype(F32)
+        for d in (4, 2, 6, 3, 5, 1, 7):
             rcopy_z(j, d).wait_recv()
             total = total + zr[j, d - 1].astype(F32)
         wg_ref[j * HD : (j + 1) * HD, :] = total
 
-    for j in range(GROUP):
-        zcopy(6 + j).wait_recv()
-        if j < 2:
-            zcopy(8 + j).start()
-        keep[2 + j] = keep[2 + j] + got[6 + j]
-        forward_heads(j)
-        for d in (4, 3, 5, 2, 6, 1, 7):
-            at_copy(j, d).start()
-        at_r[j, :, tile(t)] = at_s[j, t]
-        if j > 0:
-            reduce_x(j - 1)
-        for d in range(1, NT):
-            at_got(j, d).wait_recv()
-
-        def weight_step(zz, carry):
+    def weight_term(j, half):
+        def step(k, carry):
+            place = half * 4 + k
+            zz = lax.rem(z + distance(half, k), Z)
             term = dot(at_r[j], gall[:, tile(zz, 512)]).astype(BF)
             for xx in range(X):
-                xs[j, xx, :, tile(zz)] = term[:, xx * HD : (xx + 1) * HD]
+                xs[j, xx, :, tile(place)] = term[:, xx * HD : (xx + 1) * HD]
             return carry
 
-        lax.fori_loop(0, Z, weight_step, 0)
+        lax.fori_loop(0, 4, step, 0)
         for d in (2, 1, 3):
-            xcopy(j, d).start()
+            xcopy(j, half, d).start()
+
+    last = GROUP - 1
+    for j in range(GROUP):
+        for p in range(2):
+            qcopy(j, p).wait_recv()
+            if p == 1 and j < 2:
+                start_q(j + 2)
+            lanes = slice(p * 512, (p + 1) * 512)
+            keep[2 + j, :, lanes] = keep[2 + j, :, lanes] + got[6 + j, :, lanes]
+            forward_heads(j, p)
+            send_attended(j, p)
+        at_r[j, :, tile(t)] = at_s[j, t]
         if j == 0:
             for d in range(1, NT):
                 ag_got(d).wait_recv()
+        if j == last:
+            for i in range(last - 1):
+                for half in range(2):
+                    send_z(i, half)
         backward_heads(j)
+        for d in range(1, NT):
+            at_got(j, d).wait_recv()
+        for half in range(2):
+            weight_term(j, half)
+        if j > 0:
+            for half in range(2):
+                reduce_x(j - 1, half)
+                if j == last:
+                    send_z(j - 1, half)
 
     for c in range(KV):
         kg_ref[:, c * HD : (c + 1) * HD] = (dk[c] * scale).astype(BF)
         vg_ref[:, c * HD : (c + 1) * HD] = dv[c].astype(BF)
-    for j in range(GROUP - 1):
+    for half in range(2):
+        reduce_x(last, half)
+        send_z(last, half)
+    for j in range(last):
         reduce_z(j)
-    reduce_x(GROUP - 1)
 
     label_copy.wait_send()
-    for i in range(10):
+    for i in range(6):
         zcopy(i).wait_send()
+    for j in range(GROUP):
+        for p in range(2):
+            qcopy(j, p).wait_send()
     for i in range(4):
         for n in range(3):
             ycopy(i, n, t).wait_send()
@@ -350,18 +406,25 @@
     for j in range(GROUP):
         for d in range(1, NT):
             at_copy(j, d).wait_send()
-        for d in range(1, X):
-            xcopy(j, d).wait_send()
+        for half in range(2):
+            for d in range(1, X):
+                xcopy(j, half, d).wait_send()
     reduce_z(GROUP - 1)
     for j in range(GROUP):
         for d in range(1, Z):
             rcopy_z(j, d).wait_send()
 
 
+def deliver(*refs):
+    count = len(refs) // 2
+    for source, target in zip(refs[:count], refs[count:]):
+        target[...] = source[...]
+
+
 def local(queries, keys, values, out_grad, out_weight, lengths, dest_group, dest_offset):
     dma = pltpu.SemaphoreType.DMA
     vm = pltpu.VMEM
-    return pl.pallas_call(
+    results = pl.pallas_call(
         kernel,
         out_shape=(
             jax.ShapeDtypeStruct((T, 4096), BF),
@@ -395,13 +458,14 @@
             vm((GROUP, Z, HD, 128), BF),
             vm((GROUP, Z - 1, HD, 128), BF),
             dma((9,)),
-            dma((10,)), dma((10,)),
+            dma((6,)), dma((6,)),
+            dma((4, 2)), dma((4, 2)),
             dma((2,)),
             dma((4, 3)), dma((4, 3)),
             dma((4, 4)), dma((4, 4)),
             dma((7,)), dma((7,)),
             dma((4, 7)), dma((4, 7)),
-            dma((4, 3)), dma((4, 3)),
+            dma((4, 2, 3)), dma((4, 2, 3)),
             dma((4, 7)), dma((4, 7)),
         ],
         compiler_params=pltpu.CompilerParams(
@@ -409,6 +473,14 @@
         ),
         cost_estimate=pl.CostEstimate(flops=30_000_000_000, bytes_accessed=12_000_000, transcendentals=600_000),
     )(queries, keys, values, out_grad, out_weight, lengths, dest_group, dest_offset)
+    specs = [pl.BlockSpec((r.shape[0] // 4, r.shape[1]), lambda i: (i, 0)) for r in results]
+    return pl.pallas_call(
+        deliver,
+        grid=(4,),
+        out_shape=tuple(jax.ShapeDtypeStruct(r.shape, r.dtype) for r in results),
+        in_specs=specs,
+        out_specs=tuple(specs),
+    )(*results)
 
 
 def solution(mesh):

time: 200 us -> 170 us (0.85)
  Pallas kernels: 194 us -> 166 us
  local copies, waits for them, and re-layouts: 4.48 us -> 0 us
    pallas_call x1, Pallas kernels: 194 us -> 163 us  [local(): pl.pallas_call(kernel, out_shape=(jax.ShapeDtypeStruct((T, 4096), BF), ja...]
    unnamed x10 -> x0, local copies, waits for them, and re-layouts: 4.48 us -> none
    pallas_call x0 -> x1, Pallas kernels: none -> 3.62 us  [local(): pl.pallas_call(deliver, grid=(4,), out_shape=tuple((jax.ShapeDtypeStruct(...]
where the time goes in v2:
time: 170 us; the launch traced here: 167 us
  Pallas kernels  166 us (98%)
    pallas_call x1, Pallas kernels, local(): pl.pallas_call(kernel, out_shape=(jax.ShapeDtypeStruct((T, 4096), BF), ja...  163 us
    pallas_call x1, Pallas kernels, local(): pl.pallas_call(deliver, grid=(4,), out_shape=tuple((jax.ShapeDtypeStruct(...  3.62 us

profile of v2, /device:TPU:1, one launch (start us, length us, event | category | flops | bytes accessed | tf_op | source)
XLA Modules:
  0.0 167.0 jit_solution(2368324670659227068)
XLA Ops:
  0.6 162.8 %shard_map.111 = (bf16[128,4096]{1,0:T(8,128)(2,1)}, bf16[128,1024]{1,0:T(8,128)(2,1)}, bf16[128,1024]{1,0:T(8,128)(2,1)}, f32[512,128]{1,0:T(8,128)}) custom-call(bf16[2,128,4096]{2,1,0:T(8,128)(2,1)} %q_hbm.1, bf16[2,128,1024]{2,1,0:T(8,128)(2,1)} %k_hbm.1, bf16[2,128,1024]{2,1,0:T(8,128)(2,1)} %v_hbm.1, bf16[2,128,4096]{2,1,0:T(8,128)(2,1)} %g_hbm.1, ...), custom_call_target="tpu_custom_call" | custom-call | flops 30000001024 | bytes 12000000 | tf_op jit(solution)/shard_map/pallas_call | solution.py:427
  163.4 3.6 %shard_map.112 = (bf16[128,4096]{1,0:T(8,128)(2,1)}, bf16[128,1024]{1,0:T(8,128)(2,1)}, bf16[128,1024]{1,0:T(8,128)(2,1)}, f32[512,128]{1,0:T(8,128)}) custom-call(bf16[128,4096]{1,0:T(8,128)(2,1)} %get-tuple-element.8.refs_0_, bf16[128,1024]{1,0:T(8,128)(2,1)} %get-tuple-element.9.refs_1_, bf16[128,1024]{1,0:T(8,128)(2,1)} %get-tuple-element.10.refs_2_, ...), custom_call_target="tpu_custom_call" | custom-call | tf_op jit(solution)/shard_map/pallas_call | solution.py:477

commit v3 on v2

--- a/solution.py
+++ b/solution.py
@@ -44,9 +44,9 @@
     xin, wv, pack, mask, lab_s, lab_r,
     send, keep, got, gall,
     ag_s, ag_r, at_s, at_r, probs, outs, dk, dv,
-    xs, xr, zs, zr,
+    xs, xa, xr, zs, zr,
     in_sem, zsend, zrecv, qsend, qrecv, lsem, ysend, yrecv, csend, crecv,
-    agsend, agrecv, atsend, atrecv, xsend, xrecv, rsend, rrecv,
+    agsend, agrecv, atsend, atrecv, asend, arecv, xsend, xrecv, rsend, rrecv,
 ):
     dp = lax.axis_index("dp")
     t = lax.axis_index("tensor")
@@ -253,11 +253,25 @@
     def distance(half, k):
         return lax.rem(4 + 6 * k, Z) if half == 0 else lax.rem(3 + 2 * k, Z)
 
-    def xcopy(j, half, d):
-        lanes = slice(half * 512, (half + 1) * 512)
-        return rcopy(
-            xs.at[j, lax.rem(x + d, X), :, lanes], xr.at[j, d - 1, :, lanes],
-            xsend.at[j, half, d - 1], xrecv.at[j, half, d - 1], at_x(d),
+    def rows_of(r):
+        return slice(r * 64, (r + 1) * 64)
+
+    def lanes_of(half):
+        return slice(half * 512, (half + 1) * 512)
+
+    def beside(s):
+        return lax.rem(x + 1 + 2 * s, X)
+
+    def relay_copy(j, half, s):
+        return rcopy(
+            xs.at[j, lax.rem(x + 2, X), rows_of(s), lanes_of(half)], xa.at[j, s, :, lanes_of(half)],
+            asend.at[j, half, s], arecv.at[j, half, s], at_x(1 + 2 * s),
+        )
+
+    def xcopy(j, half, s, r):
+        return rcopy(
+            xs.at[j, beside(s), rows_of(r), lanes_of(half)], xr.at[j, s, rows_of(r), lanes_of(half)],
+            xsend.at[j, half, s, r], xrecv.at[j, half, s, r], at_x(1 + 2 * s),
         )
 
     def rcopy_z(j, d):
@@ -279,50 +293,67 @@
         lax.fori_loop(0, 4, step, 0)
 
     def forward_heads(j, p):
-        def step(m, carry):
-            c = 2 * m + p
-            query = keep[2 + j, :, tile(p * 4 + m)]
-            key = keep[0, :, tile(c)]
-            value = keep[1, :, tile(c)]
-            allowed = mask[...] > 0.5
-            score = jnp.where(allowed, dot(query, key, NTD) * scale, -1e30)
-            top = jnp.max(score, axis=-1, keepdims=True)
-            expo = jnp.exp(score - top)
-            prob = expo / jnp.sum(expo, axis=-1, keepdims=True)
-            probs[c] = prob
-            out = dot(prob.astype(BF), value)
-            out = out.astype(BF)
-            outs[c] = out
-            at_s[j, c] = out.T
+        four = range(4)
+        allowed = mask[...] > 0.5
+        scores = [
+            dot(keep[2 + j, :, tile(p * 4 + m)], keep[0, :, tile(2 * m + p)], NTD) * scale for m in four
+        ]
+        scores = [jnp.where(allowed, score, -1e30) for score in scores]
+        tops = [jnp.max(score, axis=-1, keepdims=True) for score in scores]
+        expos = [jnp.exp(scores[m] - tops[m]) for m in four]
+        sums = [jnp.sum(expo, axis=-1, keepdims=True) for expo in expos]
+        prob = [expos[m] / sums[m] for m in four]
+        out = [dot(prob[m].astype(BF), keep[1, :, tile(2 * m + p)]).astype(BF) for m in four]
+        for m in four:
+            at_s[j, 2 * m + p] = out[m].T
+        for m in four:
+            probs[2 * m + p] = prob[m]
+            outs[2 * m + p] = out[m]
+
+    def backward_heads(j):
+        def step(p, carry):
+            four = range(4)
+            heads = [2 * m + p for m in four]
+            query = [keep[2 + j, :, tile(p * 4 + m)] for m in four]
+            key = [keep[0, :, tile(c)] for c in heads]
+            value = [keep[1, :, tile(c)] for c in heads]
+            grad = [ag_r[:, tile(c * GROUP + j)] for c in heads]
+            prob = [probs[c] for c in heads]
+            delta = [
+                jnp.sum(grad[m].astype(F32) * outs[heads[m]].astype(F32), axis=-1, keepdims=True) for m in four
+            ]
+            prob_grad = [dot(grad[m], value[m], NTD) for m in four]
+            score_grad = [(prob[m] * (prob_grad[m] - delta[m])).astype(BF) for m in four]
+            query_grad = [(dot(score_grad[m], key[m]) * scale).astype(BF) for m in four]
+            key_grad = [dk[heads[m]] + dot(score_grad[m], query[m], TN) for m in four]
+            value_grad = [dv[heads[m]] + dot(prob[m].astype(BF), grad[m], TN) for m in four]
+            for m in four:
+                qg_ref[:, tile(heads[m] * GROUP + j)] = query_grad[m]
+                dk[heads[m]] = key_grad[m]
+                dv[heads[m]] = value_grad[m]
             return carry
 
-        lax.fori_loop(0, 4, step, 0, unroll=4)
-
-    def backward_heads(j):
-        def step(c, carry):
-            query = keep[2 + j, :, tile(seat(c))]
-            key = keep[0, :, tile(c)]
-            value = keep[1, :, tile(c)]
-            grad = ag_r[:, tile(c * GROUP + j)]
-            prob = probs[c]
-            delta = jnp.sum(grad.astype(F32) * outs[c].astype(F32), axis=-1, keepdims=True)
-            score_grad = (prob * (dot(grad, value, NTD) - delta)).astype(BF)
-            qg_ref[:, tile(c * GROUP + j)] = (dot(score_grad, key) * scale).astype(BF)
-            dk[c] += dot(score_grad, query, TN)
-            dv[c] += dot(prob.astype(BF), grad, TN)
-            return carry
-
-        lax.fori_loop(0, KV, step, 0, unroll=4)
+        lax.fori_loop(0, 2, step, 0)
+
+    def relay_x(j, half):
+        lanes = lanes_of(half)
+        for s in range(2):
+            relay_copy(j, half, s).wait_recv()
+            mine = xs[j, beside(s), rows_of(s), lanes].astype(F32)
+            xs[j, beside(s), rows_of(s), lanes] = (mine + xa[j, s, :, lanes].astype(F32)).astype(BF)
+            xcopy(j, half, s, s).start()
 
     def reduce_x(j, half):
-        for d in range(1, X):
-            xcopy(j, half, d).wait_recv()
+        for s in range(2):
+            xcopy(j, half, s, 1 - s).wait_recv()
+        for s in range(2):
+            xcopy(j, half, s, s).wait_recv()
 
         def step(k, carry):
             place = half * 4 + k
             total = xs[j, x, :, tile(place)].astype(F32)
-            for d in range(1, X):
-                total = total + xr[j, d - 1, :, tile(place)].astype(F32)
+            for s in range(2):
+                total = total + xr[j, s, :, tile(place)].astype(F32)
             zs[j, place] = total.astype(BF)
             return carry
 
@@ -349,8 +380,10 @@
             return carry
 
         lax.fori_loop(0, 4, step, 0)
-        for d in (2, 1, 3):
-            xcopy(j, half, d).start()
+        for s in range(2):
+            relay_copy(j, half, s).start()
+        for s in range(2):
+            xcopy(j, half, s, 1 - s).start()
 
     last = GROUP - 1
     for j in range(GROUP):
@@ -370,6 +403,9 @@
             for i in range(last - 1):
                 for half in range(2):
                     send_z(i, half)
+        if j > 0:
+            for half in range(2):
+                relay_x(j - 1, half)
         backward_heads(j)
         for d in range(1, NT):
             at_got(j, d).wait_recv()
@@ -381,6 +417,8 @@
                 if j == last:
                     send_z(j - 1, half)
 
+    for half in range(2):
+        relay_x(last, half)
     for c in range(KV):
         kg_ref[:, c * HD : (c + 1) * HD] = (dk[c] * scale).astype(BF)
         vg_ref[:, c * HD : (c + 1) * HD] = dv[c].astype(BF)
@@ -407,8 +445,10 @@
         for d in range(1, NT):
             at_copy(j, d).wait_send()
         for half in range(2):
-            for d in range(1, X):
-                xcopy(j, half, d).wait_send()
+            for s in range(2):
+                relay_copy(j, half, s).wait_send()
+                for r in range(2):
+                    xcopy(j, half, s, r).wait_send()
     reduce_z(GROUP - 1)
     for j in range(GROUP):
         for d in range(1, Z):
@@ -454,7 +494,8 @@
             vm((KV, T, HD), F32),
             vm((KV, T, HD), F32),
             vm((GROUP, X, HD, 1024), BF),
-            vm((GROUP, X - 1, HD, 1024), BF),
+            vm((GROUP, 2, HD // 2, 1024), BF),
+            vm((GROUP, 2, HD, 1024), BF),
             vm((GROUP, Z, HD, 128), BF),
             vm((GROUP, Z - 1, HD, 128), BF),
             dma((9,)),
@@ -465,7 +506,8 @@
             dma((4, 4)), dma((4, 4)),
             dma((7,)), dma((7,)),
             dma((4, 7)), dma((4, 7)),
-            dma((4, 2, 3)), dma((4, 2, 3)),
+            dma((4, 2, 2)), dma((4, 2, 2)),
+            dma((4, 2, 2, 2)), dma((4, 2, 2, 2)),
             dma((4, 7)), dma((4, 7)),
         ],
         compiler_params=pltpu.CompilerParams(

time: 170 us -> 163 us (0.959); the launches traced: 167 us -> 163 us
  Pallas kernels: 166 us -> 163 us
    pallas_call x1, Pallas kernels: 163 us -> 159 us  [local(): pl.pallas_call(kernel, out_shape=(jax.ShapeDtypeStruct((T, 4096), BF), ja...]
where the time goes in v3:
time: 163 us
  Pallas kernels  163 us (100%)
    pallas_call x1, Pallas kernels, local(): pl.pallas_call(kernel, out_shape=(jax.ShapeDtypeStruct((T, 4096), BF), ja...  159 us
    pallas_call x1, Pallas kernels, local(): pl.pallas_call(deliver, grid=(4,), out_shape=tuple((jax.ShapeDtypeStruct(...  3.62 us

profile of v3, /device:TPU:1, one launch (start us, length us, event | category | flops | bytes accessed | tf_op | source)
XLA Modules:
  0.0 163.1 jit_solution(7140194024544313005)
XLA Ops:
  0.6 158.9 %shard_map.111 = (bf16[128,4096]{1,0:T(8,128)(2,1)}, bf16[128,1024]{1,0:T(8,128)(2,1)}, bf16[128,1024]{1,0:T(8,128)(2,1)}, f32[512,128]{1,0:T(8,128)}) custom-call(bf16[2,128,4096]{2,1,0:T(8,128)(2,1)} %q_hbm.1, bf16[2,128,1024]{2,1,0:T(8,128)(2,1)} %k_hbm.1, bf16[2,128,1024]{2,1,0:T(8,128)(2,1)} %v_hbm.1, bf16[2,128,4096]{2,1,0:T(8,128)(2,1)} %g_hbm.1, ...), custom_call_target="tpu_custom_call" | custom-call | flops 30000001024 | bytes 12000000 | tf_op jit(solution)/shard_map/pallas_call | solution.py:467
  159.5 3.6 %shard_map.112 = (bf16[128,4096]{1,0:T(8,128)(2,1)}, bf16[128,1024]{1,0:T(8,128)(2,1)}, bf16[128,1024]{1,0:T(8,128)(2,1)}, f32[512,128]{1,0:T(8,128)}) custom-call(bf16[128,4096]{1,0:T(8,128)(2,1)} %get-tuple-element.8.refs_0_, bf16[128,1024]{1,0:T(8,128)(2,1)} %get-tuple-element.9.refs_1_, bf16[128,1024]{1,0:T(8,128)(2,1)} %get-tuple-element.10.refs_2_, ...), custom_call_target="tpu_custom_call" | custom-call | tf_op jit(solution)/shard_map/pallas_call | solution.py:519

commit v4 on v3

--- a/solution.py
+++ b/solution.py
@@ -20,6 +20,7 @@
 NN = (((1,), (0,)), ((), ()))
 NTD = (((1,), (1,)), ((), ()))
 TN = (((0,), (0,)), ((), ()))
+Z_STEPS = (4, 2, 6, 3, 5, 1, 7)
 PLACE = {4: 0, 2: 1, 0: 2, 6: 3, 3: 4, 5: 5, 7: 6, 1: 7}
 
 
@@ -40,6 +41,7 @@
 
 def kernel(
     q_hbm, k_hbm, v_hbm, g_hbm, w_hbm, len_ref, grp_ref, off_ref,
+    qg_hbm, kg_hbm, vg_hbm, wg_hbm,
     qg_ref, kg_ref, vg_ref, wg_ref,
     xin, wv, pack, mask, lab_s, lab_r,
     send, keep, got, gall,
@@ -47,6 +49,7 @@
     xs, xa, xr, zs, zr,
     in_sem, zsend, zrecv, qsend, qrecv, lsem, ysend, yrecv, csend, crecv,
     agsend, agrecv, atsend, atrecv, asend, arecv, xsend, xrecv, rsend, rrecv,
+    out_sem,
 ):
     dp = lax.axis_index("dp")
     t = lax.axis_index("tensor")
@@ -79,7 +82,15 @@
         pl.semaphore_signal(barrier, inc=1, device_id=peer, device_id_type=MESH)
 
     loads = []
-    for hbm, start, width in ((g_hbm, 0, 4096), (k_hbm, 4096, 1024), (v_hbm, 5120, 1024), (q_hbm, 6144, 4096)):
+    for part in range(2):
+        lanes = slice(part * 1024, 1024 + part * 3072)
+        for slot in range(2):
+            loads.append(
+                pltpu.make_async_copy(
+                    g_hbm.at[slot, :, lanes], xin.at[slot * T : (slot + 1) * T, lanes], in_sem.at[len(loads)]
+                )
+            )
+    for hbm, start, width in ((k_hbm, 4096, 1024), (v_hbm, 5120, 1024), (q_hbm, 6144, 4096)):
         for slot in range(2):
             loads.append(
                 pltpu.make_async_copy(
@@ -138,9 +149,11 @@
             pl.semaphore_wait(barrier, len(peers))
             label_copy.start()
             zcopy(0).start()
+            loads[2].wait()
+            loads[3].wait()
         if i == 1:
             zcopy(1).start()
-    for load in loads[2:8]:
+    for load in loads[4:10]:
         load.wait()
     for i in range(2):
         for half in range(2):
@@ -189,7 +202,7 @@
         if i > 0:
             forward(i - 1)
     forward(3)
-    loads[8].wait()
+    loads[10].wait()
     for i in range(4):
         for n in range(3):
             ccopy(i, n, sib_from_t(n)).wait_recv()
@@ -235,18 +248,19 @@
     dk[...] = jnp.zeros_like(dk)
     dv[...] = jnp.zeros_like(dv)
     scale = float(HD) ** (-0.5)
+    last = GROUP - 1
 
     def at_copy(j, d):
         peer = lax.rem(t + d, NT)
         return rcopy(
-            at_s.at[j, peer], at_r.at[j, :, tile(t)],
+            at_s.at[j, peer], at_r.at[j, t],
             atsend.at[j, d - 1], atrecv.at[j, d - 1], at_t(d),
         )
 
     def at_got(j, d):
         source = lax.rem(t + NT - d, NT)
         return rcopy(
-            at_s.at[j, source], at_r.at[j, :, tile(source)],
+            at_s.at[j, source], at_r.at[j, source],
             atsend.at[j, d - 1], atrecv.at[j, d - 1], at_t(d),
         )
 
@@ -310,7 +324,7 @@
             probs[2 * m + p] = prob[m]
             outs[2 * m + p] = out[m]
 
-    def backward_heads(j):
+    def backward_heads(j, p):
         def step(p, carry):
             four = range(4)
             heads = [2 * m + p for m in four]
@@ -333,7 +347,7 @@
                 dv[heads[m]] = value_grad[m]
             return carry
 
-        lax.fori_loop(0, 2, step, 0)
+        lax.fori_loop(p, p + 1, step, 0)
 
     def relay_x(j, half):
         lanes = lanes_of(half)
@@ -365,7 +379,7 @@
 
     def reduce_z(j):
         total = zs[j, PLACE[0]].astype(F32)
-        for d in (4, 2, 6, 3, 5, 1, 7):
+        for d in Z_STEPS:
             rcopy_z(j, d).wait_recv()
             total = total + zr[j, d - 1].astype(F32)
         wg_ref[j * HD : (j + 1) * HD, :] = total
@@ -374,7 +388,8 @@
         def step(k, carry):
             place = half * 4 + k
             zz = lax.rem(z + distance(half, k), Z)
-            term = dot(at_r[j], gall[:, tile(zz, 512)]).astype(BF)
+            attended = jnp.concatenate([at_r[j, source] for source in range(NT)], axis=1)
+            term = dot(attended, gall[:, tile(zz, 512)]).astype(BF)
             for xx in range(X):
                 xs[j, xx, :, tile(place)] = term[:, xx * HD : (xx + 1) * HD]
             return carry
@@ -385,43 +400,57 @@
         for s in range(2):
             xcopy(j, half, s, 1 - s).start()
 
-    last = GROUP - 1
+    def weight_chunk(j):
+        for d in range(1, NT):
+            at_got(j, d).wait_recv()
+        for half in range(2):
+            weight_term(j, half)
+
     for j in range(GROUP):
         for p in range(2):
             qcopy(j, p).wait_recv()
             if p == 1 and j < 2:
-                start_q(j + 2)
+                qcopy(j + 2, 0).start()
             lanes = slice(p * 512, (p + 1) * 512)
             keep[2 + j, :, lanes] = keep[2 + j, :, lanes] + got[6 + j, :, lanes]
             forward_heads(j, p)
             send_attended(j, p)
-        at_r[j, :, tile(t)] = at_s[j, t]
-        if j == 0:
-            for d in range(1, NT):
-                ag_got(d).wait_recv()
+            if p == 0:
+                if j == 0:
+                    for d in range(1, NT):
+                        ag_got(d).wait_recv()
+                backward_heads(j, 0)
+        at_r[j, t] = at_s[j, t]
         if j == last:
             for i in range(last - 1):
-                for half in range(2):
-                    send_z(i, half)
+                send_z(i, 0)
+                send_z(i, 1)
         if j > 0:
             for half in range(2):
                 relay_x(j - 1, half)
-        backward_heads(j)
-        for d in range(1, NT):
-            at_got(j, d).wait_recv()
-        for half in range(2):
-            weight_term(j, half)
-        if j > 0:
+        if j < last:
+            backward_heads(j, 1)
+        if j < 2:
+            qcopy(j + 2, 1).start()
+        weight_chunk(j)
+        if j > 0 and j < last:
             for half in range(2):
                 reduce_x(j - 1, half)
-                if j == last:
-                    send_z(j - 1, half)
-
+    for half in range(2):
+        reduce_x(last - 1, half)
+        send_z(last - 1, half)
     for half in range(2):
         relay_x(last, half)
+    backward_heads(last, 1)
     for c in range(KV):
         kg_ref[:, c * HD : (c + 1) * HD] = (dk[c] * scale).astype(BF)
         vg_ref[:, c * HD : (c + 1) * HD] = dv[c].astype(BF)
+    stores = [
+        pltpu.make_async_copy(held, out, out_sem.at[i])
+        for i, (held, out) in enumerate(((qg_ref, qg_hbm), (kg_ref, kg_hbm), (vg_ref, vg_hbm), (wg_ref, wg_hbm)))
+    ]
+    for store in stores[:3]:
+        store.start()
     for half in range(2):
         reduce_x(last, half)
         send_z(last, half)
@@ -450,15 +479,34 @@
                 for r in range(2):
                     xcopy(j, half, s, r).wait_send()
     reduce_z(GROUP - 1)
+    stores[3].start()
     for j in range(GROUP):
-        for d in range(1, Z):
+        for d in Z_STEPS:
             rcopy_z(j, d).wait_send()
+    for store in stores:
+        store.wait()
 
 
 def deliver(*refs):
-    count = len(refs) // 2
-    for source, target in zip(refs[:count], refs[count:]):
-        target[...] = source[...]
+    sources, targets, held = refs[:4], refs[4:8], refs[8:12]
+    load_sem, store_sem = refs[12:]
+    pieces = []
+    for n in range(4):
+        size = sources[n].shape[0] // 4
+        for part in range(4 if n == 0 else 1):
+            rows = slice(part * size, (part + 1) * size) if n == 0 else slice(0, size * 4)
+            at = len(pieces)
+            pieces.append((
+                pltpu.make_async_copy(sources[n].at[rows], held[n].at[rows], load_sem.at[at]),
+                pltpu.make_async_copy(held[n].at[rows], targets[n].at[rows], store_sem.at[at]),
+            ))
+    for load, _ in pieces:
+        load.start()
+    for load, store in pieces:
+        load.wait()
+        store.start()
+    for _, store in pieces:
+        store.wait()
 
 
 def local(queries, keys, values, out_grad, out_weight, lengths, dest_group, dest_offset):
@@ -473,8 +521,12 @@
             jax.ShapeDtypeStruct((512, 128), F32),
         ),
         in_specs=[pl.BlockSpec(memory_space=pl.ANY)] * 5 + [pl.BlockSpec(memory_space=pltpu.SMEM)] * 3,
-        out_specs=tuple([pl.BlockSpec(memory_space=pltpu.VMEM)] * 4),
+        out_specs=tuple([pl.BlockSpec(memory_space=pl.ANY)] * 4),
         scratch_shapes=[
+            vm((T, 4096), BF),
+            vm((T, 1024), BF),
+            vm((T, 1024), BF),
+            vm((512, 128), F32),
             vm((2 * T, 10240), BF),
             vm((512, 4096), BF),
             vm((2 * T, 2 * T), BF),
@@ -488,7 +540,7 @@
             vm((NT * T, 512), BF),
             vm((T, 4096), BF),
             vm((GROUP, KV, HD, T), BF),
-            vm((GROUP, HD, NT * T), BF),
+            vm((GROUP, NT, HD, T), BF),
             vm((KV, T, T), F32),
             vm((KV, T, HD), BF),
             vm((KV, T, HD), F32),
@@ -498,7 +550,7 @@
             vm((GROUP, 2, HD, 1024), BF),
             vm((GROUP, Z, HD, 128), BF),
             vm((GROUP, Z - 1, HD, 128), BF),
-            dma((9,)),
+            dma((11,)),
             dma((6,)), dma((6,)),
             dma((4, 2)), dma((4, 2)),
             dma((2,)),
@@ -509,19 +561,19 @@
             dma((4, 2, 2)), dma((4, 2, 2)),
             dma((4, 2, 2, 2)), dma((4, 2, 2, 2)),
             dma((4, 7)), dma((4, 7)),
+            dma((4,)),
         ],
         compiler_params=pltpu.CompilerParams(
             collective_id=0, has_side_effects=True, vmem_limit_bytes=60 * 2**20
         ),
         cost_estimate=pl.CostEstimate(flops=30_000_000_000, bytes_accessed=12_000_000, transcendentals=600_000),
     )(queries, keys, values, out_grad, out_weight, lengths, dest_group, dest_offset)
-    specs = [pl.BlockSpec((r.shape[0] // 4, r.shape[1]), lambda i: (i, 0)) for r in results]
     return pl.pallas_call(
         deliver,
-        grid=(4,),
         out_shape=tuple(jax.ShapeDtypeStruct(r.shape, r.dtype) for r in results),
-        in_specs=specs,
-        out_specs=tuple(specs),
+        in_specs=[pl.BlockSpec(memory_space=pl.ANY)] * 4,
+        out_specs=tuple([pl.BlockSpec(memory_space=pl.ANY)] * 4),
+        scratch_shapes=[vm(r.shape, r.dtype) for r in results] + [dma((7,)), dma((7,))],
     )(*results)
 
 

time: 163 us -> 163 us (level)
  no operation moved by 1% of the time
where the time goes in v4:
time: 163 us
  Pallas kernels  162 us (99%)
    pallas_call x1, Pallas kernels, local(): pl.pallas_call(kernel, out_shape=(jax.ShapeDtypeStruct((T, 4096), BF), ja...  160 us

profile of v4, /device:TPU:1, one launch (start us, length us, event | category | flops | bytes accessed | tf_op | source)
XLA Modules:
  0.0 162.6 jit_solution(14278777610165745948)
XLA Ops:
  0.6 159.7 %shard_map.111 = (bf16[128,4096]{1,0:T(8,128)(2,1)}, bf16[128,1024]{1,0:T(8,128)(2,1)}, bf16[128,1024]{1,0:T(8,128)(2,1)}, f32[512,128]{1,0:T(8,128)}) custom-call(bf16[2,128,4096]{2,1,0:T(8,128)(2,1)} %q_hbm.1, bf16[2,128,1024]{2,1,0:T(8,128)(2,1)} %k_hbm.1, bf16[2,128,1024]{2,1,0:T(8,128)(2,1)} %v_hbm.1, bf16[2,128,4096]{2,1,0:T(8,128)(2,1)} %g_hbm.1, ...), custom_call_target="tpu_custom_call" | custom-call | flops 30000001024 | bytes 12000000 | tf_op jit(solution)/shard_map/pallas_call | solution.py:515
  160.3 2.3 %shard_map.112 = (bf16[128,4096]{1,0:T(8,128)(2,1)}, bf16[128,1024]{1,0:T(8,128)(2,1)}, bf16[128,1024]{1,0:T(8,128)(2,1)}, f32[512,128]{1,0:T(8,128)}) custom-call(bf16[128,4096]{1,0:T(8,128)(2,1)} %get-tuple-element.8.refs_0_, bf16[128,1024]{1,0:T(8,128)(2,1)} %get-tuple-element.9.refs_1_, bf16[128,1024]{1,0:T(8,128)(2,1)} %get-tuple-element.10.refs_2_, ...), custom_call_target="tpu_custom_call" | custom-call | tf_op jit(solution)/shard_map/pallas_call | solution.py:571

commit v5 on v4

--- a/solution.py
+++ b/solution.py
@@ -78,9 +78,6 @@
     barrier = pltpu.get_barrier_semaphore()
     peers = [at_z(d) for d in range(1, Z)] + [at_x(d) for d in range(1, X)]
     peers = peers + [at_t(d) for d in range(1, NT)]
-    for peer in peers:
-        pl.semaphore_signal(barrier, inc=1, device_id=peer, device_id_type=MESH)
-
     loads = []
     for part in range(2):
         lanes = slice(part * 1024, 1024 + part * 3072)
@@ -100,7 +97,12 @@
                 )
             )
     loads.append(pltpu.make_async_copy(w_hbm, wv, in_sem.at[len(loads)]))
-    for load in loads:
+    for load in loads[:2]:
+        load.start()
+    for peer in peers:
+        pl.semaphore_signal(barrier, inc=1, device_id=peer, device_id_type=MESH)
+
+    for load in loads[2:]:
         load.start()
 
     rows = lax.broadcasted_iota(jnp.int32, (T, T), 0)
@@ -447,7 +449,10 @@
         vg_ref[:, c * HD : (c + 1) * HD] = dv[c].astype(BF)
     stores = [
         pltpu.make_async_copy(held, out, out_sem.at[i])
-        for i, (held, out) in enumerate(((qg_ref, qg_hbm), (kg_ref, kg_hbm), (vg_ref, vg_hbm), (wg_ref, wg_hbm)))
+        for i, (held, out) in enumerate((
+            (qg_ref, qg_hbm), (kg_ref, kg_hbm), (vg_ref, vg_hbm),
+            (wg_ref.at[0:384], wg_hbm.at[0:384]), (wg_ref.at[384:512], wg_hbm.at[384:512]),
+        ))
     ]
     for store in stores[:3]:
         store.start()
@@ -456,6 +461,7 @@
         send_z(last, half)
     for j in range(last):
         reduce_z(j)
+    stores[3].start()
 
     label_copy.wait_send()
     for i in range(6):
@@ -479,7 +485,7 @@
                 for r in range(2):
                     xcopy(j, half, s, r).wait_send()
     reduce_z(GROUP - 1)
-    stores[3].start()
+    stores[4].start()
     for j in range(GROUP):
         for d in Z_STEPS:
             rcopy_z(j, d).wait_send()
@@ -561,7 +567,7 @@
             dma((4, 2, 2)), dma((4, 2, 2)),
             dma((4, 2, 2, 2)), dma((4, 2, 2, 2)),
             dma((4, 7)), dma((4, 7)),
-            dma((4,)),
+            dma((5,)),
         ],
         compiler_params=pltpu.CompilerParams(
             collective_id=0, has_side_effects=True, vmem_limit_bytes=60 * 2**20

time: 163 us -> 162 us (level)
  no operation moved by 1% of the time
where the time goes in v5:
time: 162 us
  Pallas kernels  161 us (99%)
    pallas_call x1, Pallas kernels, local(): pl.pallas_call(kernel, out_shape=(jax.ShapeDtypeStruct((T, 4096), BF), ja...  159 us

profile of v5, /device:TPU:1, one launch (start us, length us, event | category | flops | bytes accessed | tf_op | source)
XLA Modules:
  0.0 162.1 jit_solution(16164559056492617182)
XLA Ops:
  0.6 159.2 %shard_map.111 = (bf16[128,4096]{1,0:T(8,128)(2,1)}, bf16[128,1024]{1,0:T(8,128)(2,1)}, bf16[128,1024]{1,0:T(8,128)(2,1)}, f32[512,128]{1,0:T(8,128)}) custom-call(bf16[2,128,4096]{2,1,0:T(8,128)(2,1)} %q_hbm.1, bf16[2,128,1024]{2,1,0:T(8,128)(2,1)} %k_hbm.1, bf16[2,128,1024]{2,1,0:T(8,128)(2,1)} %v_hbm.1, bf16[2,128,4096]{2,1,0:T(8,128)(2,1)} %g_hbm.1, ...), custom_call_target="tpu_custom_call" | custom-call | flops 30000001024 | bytes 12000000 | tf_op jit(solution)/shard_map/pallas_call | solution.py:521
  159.8 2.3 %shard_map.112 = (bf16[128,4096]{1,0:T(8,128)(2,1)}, bf16[128,1024]{1,0:T(8,128)(2,1)}, bf16[128,1024]{1,0:T(8,128)(2,1)}, f32[512,128]{1,0:T(8,128)}) custom-call(bf16[128,4096]{1,0:T(8,128)(2,1)} %get-tuple-element.8.refs_0_, bf16[128,1024]{1,0:T(8,128)(2,1)} %get-tuple-element.9.refs_1_, bf16[128,1024]{1,0:T(8,128)(2,1)} %get-tuple-element.10.refs_2_, ...), custom_call_target="tpu_custom_call" | custom-call | tf_op jit(solution)/shard_map/pallas_call | solution.py:577
